TPU v7x, 32 devices: a whole 2x2x4 slice. The times are simulated.
32 devices in a mesh: col: 4 (over z), depth: 8 (over y, x, core).
Axes of the slice: x: 2, y: 2, z: 4, core: 2. Of those that a mesh axis runs over, the one named last changes fastest.
Arguments:
- volume: bfloat16 [128, 256, 512], P('depth', None, 'col'), may hold values from -6 to 6
- tf_index: int32 [128, 256, 512], P('depth', None, 'col'), may hold values from 0 to 255
- tf_table: bfloat16 [4, 256], replicated, may hold values from 0 to 1, as said below
Outputs:
- frame: float32 [4, 256, 512], P(None, 'depth', 'col')
Inputs may be any that keep to these rules, and one draw needn't show every extreme that they name: Rows 0 to 2 of tf_table are positive colours; row 3 is a positive extinction.
All inputs are finite; a program needn't handle non-finite values.
Results may differ from a plain program's by a relative error of at most 0.005.
Values may be sent and summed in bfloat16 or wider, within the bound.
A program may use at most 128 MiB of HBM per device.

v0:
```python
import functools

import jax
import jax.numpy as jnp
from jax import lax
from jax.experimental import pallas as pl
from jax.experimental.pallas import tpu as pltpu
from jax.sharding import PartitionSpec as P

LIGHT = (0.75 * 0.36, 0.75 * 0.48, 0.75 * 0.8)
LOG2E = 1.4426950408889634
LN2 = 0.6931471805599453
PAD = 8


def one_minus_exp(x):
    series = x * (1.0 - x * (0.5 - x * (1.0 / 6.0 - x * (1.0 / 24.0 - x * (1.0 / 120.0)))))
    return jnp.where(x < 0.125, series, 1.0 - jnp.exp(-x))


def kernel(n, m, vol_hbm, idx_hbm, table_hbm, out, vol, idx, table, load_sem, pre, fvol, dx, part, recv, edge, zlo, zhi, from_left, from_right,
           send_sem, recv_sem, halo_send, halo_recv):
    depth, rows, cols = vol.shape
    rb = rows // n
    me = lax.axis_index("depth")
    mine = lax.axis_index("col")

    loads = [pltpu.make_async_copy(src, dst, load_sem.at[i]) for i, (src, dst) in
             enumerate(((table_hbm, table), (vol_hbm, vol), (idx_hbm, idx)))]
    for load in loads:
        load.start()

    barrier = pltpu.get_barrier_semaphore()

    def greet(k, c):
        pl.semaphore_signal(barrier, inc=1, device_id={"depth": lax.rem(me + 1 + k, n)},
                            device_id_type=pl.DeviceIdType.MESH)
        return c

    lax.fori_loop(0, n - 1, greet, 0)
    for there, side in ((mine > 0, -1), (mine < m - 1, 1)):
        @pl.when(there)
        def _():
            pl.semaphore_signal(barrier, inc=1, device_id={"col": mine + side},
                                device_id_type=pl.DeviceIdType.MESH)

    def halo_copy(k, src, dst, axis, to):
        return pltpu.make_async_remote_copy(
            src_ref=src, dst_ref=dst, send_sem=halo_send.at[k], recv_sem=halo_recv.at[k],
            device_id={axis: to}, device_id_type=pl.DeviceIdType.MESH)

    along_z = ((me > 0, me < n - 1, halo_copy(0, vol.at[0], zhi, "depth", me - 1), zhi),
               (me < n - 1, me > 0, halo_copy(1, vol.at[depth - 1], zlo, "depth", me + 1), zlo))
    along_x = ((mine > 0, mine < m - 1, halo_copy(2, edge, from_right, "col", mine - 1), from_right),
               (mine < m - 1, mine > 0, halo_copy(3, edge, from_left, "col", mine + 1), from_left))

    def send(halos):
        for sends, _, copy, _ in halos:
            pl.when(sends)(copy.start)

    def receive(halos):
        for sends, receives, copy, landed in halos:
            pl.when(sends)(copy.wait_send)
            pl.when(receives)(copy.wait_recv)

            @pl.when(jnp.logical_not(receives))
            def _():
                landed[...] = jnp.zeros_like(landed)

    loads[1].wait()
    r_i = lax.broadcasted_iota(jnp.int32, (cols, cols), 0)
    c_i = lax.broadcasted_iota(jnp.int32, (cols, cols), 1)
    diff = jnp.where(r_i == c_i + 1, 1.0, 0.0) - jnp.where(r_i == c_i - 1, 1.0, 0.0)
    diff = diff.astype(jnp.bfloat16)
    zero = jnp.zeros((PAD, cols), jnp.float32)

    def pick(z, total):
        at = jnp.where((r_i == cols - 1) & (c_i == z), 1.0, 0.0)
        at = at + jnp.where((r_i == 0) & (c_i == depth + z), 1.0, 0.0)
        return total + jnp.dot(vol[z], at.astype(jnp.bfloat16), preferred_element_type=jnp.float32)

    edges = lax.fori_loop(0, depth, pick, jnp.zeros((rows, cols), jnp.float32), unroll=True)
    fold = cols // (2 * depth)
    short = rows // fold
    packed = edges[:short]
    for i in range(1, fold):
        packed = packed + pltpu.roll(edges[i * short:(i + 1) * short], 2 * depth * i, 1)
    edge[...] = packed.astype(jnp.bfloat16)
    neighbours = (mine > 0).astype(jnp.int32) + (mine < m - 1).astype(jnp.int32)
    pl.semaphore_wait(barrier, n - 1 + neighbours)
    send(along_z)

    send(along_x)

    loads[0].wait()
    entries = table[...].astype(jnp.float32)
    sigma = entries[3:4]
    alpha = one_minus_exp(sigma)
    logs = [jnp.log(jnp.maximum(v, 1.2e-38)) * LOG2E
            for v in [entries[c:c + 1] * alpha for c in range(3)] + [sigma * LOG2E]]
    most = [jnp.max(v, axis=1, keepdims=True) for v in logs]
    least = [jnp.min(v, axis=1, keepdims=True) for v in logs]
    middle = [0.5 * (a + b) for a, b in zip(most, least)]
    grain = [jnp.maximum(a - b, 1e-3) * (1.0 / 65532.0) for a, b in zip(most, least)]
    place = [(v - o) / g for v, o, g in zip(logs, middle, grain)]

    def word(upper, lower):
        lower = jnp.floor(lower + 0.5)
        upper = jnp.floor(upper - lower * (1.0 / 65536.0) + 0.5)
        return upper.astype(jnp.int32) * 65536 + lower.astype(jnp.int32)

    sub = 8
    words = (word(place[0], place[1]), word(place[2], place[3]))
    low = [jnp.broadcast_to(t[:, :128], (sub, 128)) for t in words]
    high = [jnp.broadcast_to(t[:, 128:], (sub, 128)) for t in words]
    spread = [jnp.broadcast_to(g * (1.0 / 65536.0), (sub, cols)) for g in grain]
    sigma_middle = jnp.broadcast_to(middle[3], (sub, cols))
    scale = [jnp.broadcast_to(jnp.exp2(o), (sub, cols)) for o in middle[:3]]

    def search(word, z, r0):
        label = idx[z, pl.ds(r0, sub)]
        lane = label & 127
        return jnp.where(label < 128, jnp.take_along_axis(low[word], lane, axis=1),
                         jnp.take_along_axis(high[word], lane, axis=1))

    loads[2].wait()

    early = depth * 12 // 16

    def widen(z, c):
        def rows_of(i, c):
            r0 = pl.multiple_of(i * sub, sub)
            pre[z, pl.ds(r0, sub)] = search(0, z, r0)
            return c

        @pl.when(z < early)
        def _():
            lax.fori_loop(0, rows // sub, rows_of, 0, unroll=True)

        v = vol[z]
        fvol[z + 1, :PAD] = zero
        fvol[z + 1, PAD + rows:] = zero
        fvol[z + 1, PAD:PAD + rows] = v.astype(jnp.float32)
        return c

    lax.fori_loop(0, depth, widen, 0)
    receive(along_x)
    lane = lax.broadcasted_iota(jnp.int32, (short, cols), 1)
    packed = jnp.where(lax.rem(lane, 2 * depth) < depth, from_left[...].astype(jnp.float32),
                       from_right[...].astype(jnp.float32))
    halo = [packed] + [pltpu.roll(packed, cols - 2 * depth * i, 1) for i in range(1, fold)]
    halo = jnp.concatenate(halo, 0).astype(jnp.bfloat16)

    def stage(z, c):
        v = vol[z]
        ends = jnp.where((c_i == cols - 1) & (r_i == depth + z), 1.0, 0.0)
        ends = ends - jnp.where((c_i == 0) & (r_i == z), 1.0, 0.0)
        weights = jnp.concatenate([diff, ends.astype(jnp.bfloat16)], 0)
        both = jnp.concatenate([v, halo], 1)
        dx[z] = jnp.dot(both, weights, preferred_element_type=jnp.float32)
        return c

    lax.fori_loop(0, depth, stage, 0, unroll=8)
    receive(along_z)
    fvol[0, PAD:PAD + rows] = zlo[...].astype(jnp.float32)
    fvol[depth + 1, PAD:PAD + rows] = zhi[...].astype(jnp.float32)

    def block(r0):
        def step(z, carry, known):
            acc0, acc1, acc2, s = carry
            at = pl.multiple_of(PAD + r0, 8)
            gx = dx[z, pl.ds(pl.multiple_of(r0, 8), sub)]
            gy = fvol[z + 1, pl.ds(at + 1, sub)] - fvol[z + 1, pl.ds(at - 1, sub)]
            gz = fvol[z + 2, pl.ds(at, sub)] - fvol[z, pl.ds(at, sub)]
            facing = gx * LIGHT[0] + gy * LIGHT[1] + gz * LIGHT[2]
            inv = lax.rsqrt(gx * gx + gy * gy + (gz * gz + 4.0))
            shade = 0.25 + jnp.abs(facing) * inv
            r1 = pl.multiple_of(r0, 8)
            first = pre[z, pl.ds(r1, sub)] if known else search(0, z, r1)
            second = search(1, z, r1)
            codes = (first, first << 16, second, second << 16)
            code0, code1, code2, code3 = [c.astype(jnp.float32) * g for c, g in zip(codes, spread)]
            return (acc0 + jnp.exp2(code0 + s) * shade, acc1 + jnp.exp2(code1 + s) * shade,
                    acc2 + jnp.exp2(code2 + s) * shade, s - jnp.exp2(code3 + sigma_middle))

        init = tuple(jnp.zeros((sub, cols), jnp.float32) for _ in range(4))
        sums = lax.fori_loop(0, early, functools.partial(step, known=True), init, unroll=True)
        sums = lax.fori_loop(early, depth, functools.partial(step, known=False), sums, unroll=True)
        return tuple(a * g for a, g in zip(sums[:3], scale)) + sums[3:]

    def compute(d):
        tiles = [block(d * rb + sub * i) for i in range(rb // sub)]
        return jnp.concatenate([t[c] for c in range(4) for t in tiles], 0).astype(jnp.bfloat16)

    def copy(k):
        return pltpu.make_async_remote_copy(
            src_ref=part.at[k], dst_ref=recv.at[k],
            send_sem=send_sem.at[k], recv_sem=recv_sem.at[k],
            device_id={"depth": lax.rem(me + 1 + k, n)},
            device_id_type=pl.DeviceIdType.MESH)

    def work(k, c):
        part[k] = compute(lax.rem(me + 1 + k, n))
        copy(k).start()
        return c

    lax.fori_loop(0, n - 1, work, 0)
    recv[n - 1] = compute(me)

    def arrive(k, c):
        copy(k).wait()
        return c

    lax.fori_loop(0, n - 1, arrive, 0)

    def over(j, carry):
        color, s = carry
        piece = recv[lax.rem(me - j - 1 + 2 * n, n)].astype(jnp.float32)
        t = jnp.exp2(s)
        color = tuple(color[c] + t * piece[c * rb:(c + 1) * rb] for c in range(3))
        return color, s + piece[3 * rb:]

    init = jnp.zeros((rb, cols), jnp.float32)
    color, s = lax.fori_loop(0, n, over, ((init,) * 3, init))
    for c in range(3):
        out[c] = color[c]
    out[3] = one_minus_exp(s * -LN2)


def on_device(volume, tf_index, tf_table):
    depth, rows, cols = volume.shape
    n = lax.axis_size("depth")
    m = lax.axis_size("col")
    vm = pl.BlockSpec(memory_space=pltpu.VMEM)
    rb = rows // n
    return pl.pallas_call(
        functools.partial(kernel, n, m),
        out_shape=jax.ShapeDtypeStruct((4, rb, cols), jnp.float32),
        in_specs=[pl.BlockSpec(memory_space=pltpu.HBM)] * 3,
        out_specs=vm,
        scratch_shapes=[
            pltpu.VMEM(volume.shape, volume.dtype),
            pltpu.VMEM(tf_index.shape, tf_index.dtype),
            pltpu.VMEM(tf_table.shape, tf_table.dtype),
            pltpu.SemaphoreType.DMA((3,)),
            pltpu.VMEM(tf_index.shape, jnp.int32),
            pltpu.VMEM((depth + 2, rows + 2 * PAD, cols), jnp.float32),
            pltpu.VMEM((depth, rows, cols), jnp.float32),
            pltpu.VMEM((n, 4 * rb, cols), jnp.bfloat16),
            pltpu.VMEM((n, 4 * rb, cols), jnp.bfloat16),
            pltpu.VMEM((2 * rows * depth // cols, cols), jnp.bfloat16),
            *[pltpu.VMEM((rows, cols), jnp.bfloat16)] * 2,
            *[pltpu.VMEM((2 * rows * depth // cols, cols), jnp.bfloat16)] * 2,
            pltpu.SemaphoreType.DMA((n - 1,)),
            pltpu.SemaphoreType.DMA((n - 1,)),
            pltpu.SemaphoreType.DMA((4,)),
            pltpu.SemaphoreType.DMA((4,)),
        ],
        compiler_params=pltpu.CompilerParams(
            collective_id=0, has_side_effects=True, vmem_limit_bytes=62 * 1024 * 1024),
    )(volume, tf_index, tf_table)


def solution(mesh):
    in_specs = (P("depth", None, "col"), P("depth", None, "col"), P())
    out_specs = P(None, "depth", "col")
    return jax.shard_map(
        on_device, mesh=mesh, in_specs=in_specs, out_specs=out_specs, check_vma=False
    )
```

profile of v0, /device:TPU:0, one launch (start us, length us, event | category | flops | bytes accessed | tf_op | source)
XLA Modules:
  0.0 16.2 jit_solution(10602455825211123881)
XLA Ops:
  0.0 14.7 %shard_map.37 = f32[4,32,128]{2,1,0:T(8,128)} custom-call(bf16[16,256,128]{2,1,0:T(8,128)(2,1)} %vol_hbm.1, s32[16,256,128]{2,1,0:T(8,128)} %idx_hbm.1, bf16[4,256]{1,0:T(4,128)(2,1)} %table_hbm.1), custom_call_target="tpu_custom_call" | custom-call | tf_op jit(solution)/shard_map/pallas_call | solution.py:236
  14.7 1.5 %copy.5 = f32[4,32,128]{2,1,0:T(8,128)} copy(f32[4,32,128]{2,1,0:T(8,128)} %shard_map.37) | data formatting | bytes 131072
where the time goes:
time: 16.3 us; the launch traced here: 16.2 us
  Pallas kernels  14.7 us (90%)
  local copies, waits for them, and re-layouts  1.47 us (9%)
    pallas_call x1, Pallas kernels, on_device(): pl.pallas_call(functools.partial(kernel, n, m), out_shape=jax.ShapeDtypeS...  14.7 us
    unnamed x1, local copies, waits for them, and re-layouts  1.47 us

commit v1 on v0

--- a/solution.py
+++ b/solution.py
@@ -257,7 +257,7 @@
             pltpu.SemaphoreType.DMA((4,)),
         ],
         compiler_params=pltpu.CompilerParams(
-            collective_id=0, has_side_effects=True, vmem_limit_bytes=62 * 1024 * 1024),
+            collective_id=0, has_side_effects=True, vmem_limit_bytes=53 * 1024 * 1024),
     )(volume, tf_index, tf_table)
 
 

time: 16.3 us -> 15.5 us (0.951)
  Pallas kernels: 14.7 us -> 14 us
    pallas_call x1, Pallas kernels: 14.7 us -> 14 us  [on_device(): pl.pallas_call(functools.partial(kernel, n, m), out_shape=jax.ShapeDtypeS...]
    unnamed x1 -> x3, local copies, waits for them, and re-layouts: 1.47 us -> 1.31 us
where the time goes in v1:
time: 15.5 us; the launch traced here: 15.4 us
  Pallas kernels  14 us (90%)
  local copies, waits for them, and re-layouts  1.31 us (8%)
    pallas_call x1, Pallas kernels, on_device(): pl.pallas_call(functools.partial(kernel, n, m), out_shape=jax.ShapeDtypeS...  14 us
    unnamed x3, local copies, waits for them, and re-layouts  1.31 us

profile of v1, /device:TPU:0, one launch (start us, length us, event | category | flops | bytes accessed | tf_op | source)
XLA Modules:
  0.0 15.4 jit_solution(18258022932142790431)
XLA Ops:
  0.0 0.0 copy-start
  0.0 0.7 %copy-done = bf16[4,256]{1,0:T(4,128)(2,1)S(1)} copy-done((bf16[4,256]{1,0:T(4,128)(2,1)S(1)}, bf16[4,256]{1,0:T(4,128)(2,1)}, u32[]{:S(2)}) %copy-start) | copy-done | bytes 2072
  0.7 14.0 %shard_map.37 = f32[4,32,128]{2,1,0:T(8,128)S(1)} custom-call(bf16[16,256,128]{2,1,0:T(8,128)(2,1)} %vol_hbm.1, s32[16,256,128]{2,1,0:T(8,128)} %idx_hbm.1, bf16[4,256]{1,0:T(4,128)(2,1)S(1)} %copy-done), custom_call_target="tpu_custom_call" | custom-call | tf_op jit(solution)/shard_map/pallas_call | solution.py:236
  14.7 0.6 %copy.5 = f32[4,32,128]{2,1,0:T(8,128)} copy(f32[4,32,128]{2,1,0:T(8,128)S(1)} %shard_map.37) | data formatting | bytes 131072
Async XLA Ops:
  0.0 0.7 %copy-start = (bf16[4,256]{1,0:T(4,128)(2,1)S(1)}, bf16[4,256]{1,0:T(4,128)(2,1)}, u32[]{:S(2)}) copy-start(bf16[4,256]{1,0:T(4,128)(2,1)} %table_hbm.1) | copy-start | bytes 6148

commit v2 on v1

v2 whole, which is shorter than its diff:
```python
import functools

import jax
import jax.numpy as jnp
from jax import lax
from jax.experimental import pallas as pl
from jax.experimental.pallas import tpu as pltpu
from jax.sharding import PartitionSpec as P

LIGHT = (0.75 * 0.36, 0.75 * 0.48, 0.75 * 0.8)
LOG2E = 1.4426950408889634
LN2 = 0.6931471805599453
PAD = 8
SUB = 8
UNIT = 32
MESH = pl.DeviceIdType.MESH


def one_minus_exp(x):
    series = x * (1.0 - x * (0.5 - x * (1.0 / 6.0 - x * (1.0 / 24.0 - x * (1.0 / 120.0)))))
    return jnp.where(x < 0.125, series, 1.0 - jnp.exp(-x))


def place_of(k, mine, count):
    if count & (count - 1):
        return lax.rem(mine + 1 + k, count)
    mask, out = count - 1 - k, 0
    for i in range(count.bit_length() - 1):
        out = out + lax.rem(lax.div(mine, 1 << i) + lax.div(mask, 1 << i), 2) * (1 << i)
    return out


def take(row, lane):
    return jnp.take_along_axis(row, lane, axis=1, mode="promise_in_bounds")


def kernel(n, m, vol_hbm, idx_hbm, table_hbm, out, vol, idx, table, load_sem, fvol, weight, across, slope, square, base, depths,
           part, recv, edge, zlo, zhi, from_left, from_right, halo, send_sem, recv_sem, halo_send, halo_recv):
    depth, rows, cols = vol.shape
    rb = rows // n
    group = UNIT // rb
    units = rows // UNIT
    tiles = UNIT // SUB
    me = lax.axis_index("depth")
    mine = lax.axis_index("col")
    my_unit = lax.div(me, group)

    def load_labels(k):
        at = pl.ds(pl.multiple_of(place_of(k, my_unit, units) * UNIT, UNIT), UNIT)
        return pltpu.make_async_copy(idx_hbm.at[:, at], idx.at[:, at], load_sem.at[2 + k])

    loads = [pltpu.make_async_copy(src, dst, load_sem.at[i]) for i, (src, dst) in
             enumerate(((table_hbm, table), (vol_hbm, vol)))]
    for load in loads:
        load.start()
    lax.fori_loop(0, units, lambda k, c: (load_labels(k).start(), c)[1], 0)

    barrier = pltpu.get_barrier_semaphore()

    def greet(k, c):
        pl.semaphore_signal(barrier, inc=1, device_id={"depth": lax.rem(me + 1 + k, n)}, device_id_type=MESH)
        return c

    lax.fori_loop(0, n - 1, greet, 0)
    for there, side in ((mine > 0, -1), (mine < m - 1, 1)):
        @pl.when(there)
        def _():
            pl.semaphore_signal(barrier, inc=1, device_id={"col": mine + side}, device_id_type=MESH)

    def halo_copy(k, src, dst, axis, to):
        return pltpu.make_async_remote_copy(
            src_ref=src, dst_ref=dst, send_sem=halo_send.at[k], recv_sem=halo_recv.at[k],
            device_id={axis: to}, device_id_type=MESH)

    halos = ((mine > 0, mine < m - 1, halo_copy(2, edge, from_right, "col", mine - 1), from_right),
             (mine < m - 1, mine > 0, halo_copy(3, edge, from_left, "col", mine + 1), from_left),
             (me > 0, me < n - 1, halo_copy(0, vol.at[0], zhi, "depth", me - 1), zhi),
             (me < n - 1, me > 0, halo_copy(1, vol.at[depth - 1], zlo, "depth", me + 1), zlo))

    r_i = lax.broadcasted_iota(jnp.int32, (cols, cols), 0)
    c_i = lax.broadcasted_iota(jnp.int32, (cols, cols), 1)
    diff = jnp.where(r_i == c_i + 1, 1.0, 0.0) - jnp.where(r_i == c_i - 1, 1.0, 0.0)
    diff = diff.astype(jnp.bfloat16)
    zero = jnp.zeros((PAD, cols), jnp.float32)

    loads[0].wait()
    entries = table[...].astype(jnp.float32)
    sigma = entries[3:4]
    alpha = one_minus_exp(sigma)
    logs = [jnp.log(jnp.maximum(v, 1.2e-38)) * LOG2E
            for v in [entries[c:c + 1] * alpha for c in range(3)] + [sigma * LOG2E]]
    most = [jnp.max(v, axis=1, keepdims=True) for v in logs]
    least = [jnp.min(v, axis=1, keepdims=True) for v in logs]
    middle = [0.5 * (a + b) for a, b in zip(most, least)]
    grain = [jnp.maximum(a - b, 1e-3) * (1.0 / 65532.0) for a, b in zip(most, least)]
    place = [(v - o) / g for v, o, g in zip(logs, middle, grain)]

    def word(upper, lower):
        lower = jnp.floor(lower + 0.5)
        upper = jnp.floor(upper - lower * (1.0 / 65536.0) + 0.5)
        return upper.astype(jnp.int32) * 65536 + lower.astype(jnp.int32)

    words = (word(place[0], place[1]), word(place[2], place[3]))
    low = [jnp.broadcast_to(t[:, :128], (SUB, 128)) for t in words]
    high = [jnp.broadcast_to(t[:, 128:], (SUB, 128)) for t in words]
    spread = [jnp.broadcast_to(g * (1.0 / 65536.0), (SUB, cols)) for g in grain]
    sigma_middle = jnp.broadcast_to(middle[3], (SUB, cols))
    scale = [jnp.broadcast_to(jnp.exp2(o), (SUB, cols)) for o in middle[:3]]

    loads[1].wait()

    def pick(z, total):
        at = jnp.where((r_i == cols - 1) & (c_i == z), 1.0, 0.0)
        at = at + jnp.where((r_i == 0) & (c_i == depth + z), 1.0, 0.0)
        return total + jnp.dot(vol[z], at.astype(jnp.bfloat16), preferred_element_type=jnp.float32)

    edges = lax.fori_loop(0, depth, pick, jnp.zeros((rows, cols), jnp.float32), unroll=True)
    edge[...] = edges.astype(jnp.bfloat16)

    def widen(z, c):
        fvol[z + 1, :PAD] = zero
        fvol[z + 1, PAD + rows:] = zero
        fvol[z + 1, PAD:PAD + rows] = vol[z].astype(jnp.float32)
        return c

    lax.fori_loop(0, depth, widen, 0)

    def look(k, c):
        @pl.when(k == 1)
        def _():
            neighbours = (mine > 0).astype(jnp.int32) + (mine < m - 1).astype(jnp.int32)
            pl.semaphore_wait(barrier, n - 1 + neighbours)
            for sends, _, copy, _ in halos:
                pl.when(sends)(copy.start)

        load_labels(k).wait()
        u0 = pl.multiple_of(place_of(k, my_unit, units) * UNIT, UNIT)
        sums = [[jnp.zeros((SUB, cols), jnp.float32) for _ in range(4)] for _ in range(tiles)]
        def decode(z, i, first, second, gxs):
            r = slice(i * SUB, (i + 1) * SUB)
            acc0, acc1, acc2, s = sums[i]
            codes = (first, first << 16, second, second << 16)
            code0, code1, code2, code3 = [v.astype(jnp.float32) * g for v, g in zip(codes, spread)]
            w0, w1, w2 = jnp.exp2(code0 + s), jnp.exp2(code1 + s), jnp.exp2(code2 + s)
            weight[k, 0, z, r], weight[k, 1, z, r], weight[k, 2, z, r] = w0, w1, w2
            sums[i] = [acc0 + w0, acc1 + w1, acc2 + w2, s - jnp.exp2(code3 + sigma_middle)]
            at = pl.multiple_of(PAD + u0 + i * SUB, SUB)
            gy = fvol[z + 1, pl.ds(at + 1, SUB)] - fvol[z + 1, pl.ds(at - 1, SUB)]
            facing = gy * LIGHT[1]
            norm = gy * gy + 4.0
            if 0 < z < depth - 1:
                gz = fvol[z + 2, pl.ds(at, SUB)] - fvol[z, pl.ds(at, SUB)]
                facing = facing + gz * LIGHT[2]
                norm = norm + gz * gz
            across[k, z, r] = gxs[r]
            slope[k, z, r] = facing
            square[k, z, r] = norm

        places = [(z, i) for z in range(depth) for i in range(tiles)]
        gx = [jnp.dot(vol[z, pl.ds(u0, UNIT)], diff, preferred_element_type=jnp.float32) for z in range(depth)]
        got, busy, open_at = {}, [3, 0], [None, None]
        fresh = iter(places)
        decoded = 0
        while decoded < len(places):
            side = 1 if busy[1] <= busy[0] else 0
            if open_at[side] is None:
                place = next(fresh, None)
                if place is None:
                    side = 1 - side
                    if open_at[side] is None:
                        break
                else:
                    z, i = place
                    label = idx[z, pl.ds(u0 + i * SUB, SUB)]
                    open_at[side] = (place, label & 127, label < 128, [])
                    busy[side] += 1 - side
            place, lane, lower, words = open_at[side]
            words.append(take((low[1], high[1], low[0], high[0])[len(words)], lane))
            busy[side] += 1
            if len(words) == 4:
                got[place] = jnp.where(lower, words[2], words[3]), jnp.where(lower, words[0], words[1])
                open_at[side] = None
            while decoded < len(places) and places[decoded] in got:
                z, i = places[decoded]
                decode(z, i, *got[z, i], gx[z])
                decoded += 1
        for i in range(tiles):
            r = slice(i * SUB, (i + 1) * SUB)
            for c3 in range(3):
                base[k, c3, r] = sums[i][c3] * 0.25
            depths[k, r] = sums[i][3]
        return c

    lax.fori_loop(0, units, look, 0)

    for sends, receives, copy, landed in halos:
        pl.when(sends)(copy.wait_send)
        pl.when(receives)(copy.wait_recv)

        @pl.when(jnp.logical_not(receives))
        def _():
            landed[...] = jnp.zeros_like(landed)

    fvol[0, PAD:PAD + rows] = zlo[...].astype(jnp.float32)
    fvol[depth + 1, PAD:PAD + rows] = zhi[...].astype(jnp.float32)
    lane = lax.broadcasted_iota(jnp.int32, (rows, cols), 1)
    halo[...] = jnp.where(lane < depth, -from_left[...].astype(jnp.float32),
                          jnp.where(lane < 2 * depth, from_right[...].astype(jnp.float32), 0.0))
    lane = lax.broadcasted_iota(jnp.int32, (SUB, cols), 1)

    def copy(k, j):
        to = place_of(k, my_unit, units) * group + j
        return to, pltpu.make_async_remote_copy(
            src_ref=part.at[k, j], dst_ref=recv.at[me], send_sem=send_sem.at[k, j], recv_sem=recv_sem.at[me],
            device_id={"depth": to}, device_id_type=MESH)

    def shade(k, c):
        u0 = pl.multiple_of(place_of(k, my_unit, units) * UNIT, UNIT)
        sums = [[base[k, c3, i * SUB:(i + 1) * SUB] for c3 in range(3)] for i in range(tiles)]
        ends = [halo[pl.ds(u0 + i * SUB, SUB)] for i in range(tiles)]
        for z in range(depth):
            outer = jnp.where(lane == 0, z, jnp.where(lane == cols - 1, depth + z, cols - 1))
            for i in range(tiles):
                r = slice(i * SUB, (i + 1) * SUB)
                gx = across[k, z, r] + take(ends[i], outer)
                facing = slope[k, z, r] + gx * LIGHT[0]
                norm = square[k, z, r] + gx * gx
                if z == 0 or z == depth - 1:
                    at = pl.multiple_of(PAD + u0 + i * SUB, SUB)
                    gz = fvol[z + 2, pl.ds(at, SUB)] - fvol[z, pl.ds(at, SUB)]
                    facing = facing + gz * LIGHT[2]
                    norm = norm + gz * gz
                lit = jnp.abs(facing) * lax.rsqrt(norm)
                sums[i] = [a + weight[k, c3, z, r] * lit for c3, a in enumerate(sums[i])]
        color = [jnp.concatenate([sums[i][c3] * scale[c3] for i in range(tiles)], 0) for c3 in range(3)]
        color.append(depths[k])
        for j in range(group):
            part[k, j] = jnp.concatenate([v[j * rb:(j + 1) * rb] for v in color], 0).astype(jnp.bfloat16)
            to, send = copy(k, j)
            pl.when(to != me)(send.start)
        return c

    lax.fori_loop(0, units, shade, 0)
    recv[me] = part[units - 1, lax.rem(me, group)]

    def arrive(k, c):
        @pl.when(k != me)
        def _():
            pltpu.make_async_remote_copy(
                src_ref=part.at[0, 0], dst_ref=recv.at[k], send_sem=send_sem.at[0, 0], recv_sem=recv_sem.at[k],
                device_id={"depth": k}, device_id_type=MESH).wait_recv()
        return c

    lax.fori_loop(0, n, arrive, 0)

    def over(j, carry):
        color, s = carry
        piece = recv[j].astype(jnp.float32)
        t = jnp.exp2(s)
        color = tuple(color[c] + t * piece[c * rb:(c + 1) * rb] for c in range(3))
        return color, s + piece[3 * rb:]

    init = jnp.zeros((rb, cols), jnp.float32)
    color, s = lax.fori_loop(0, n, over, ((init,) * 3, init), unroll=8)
    for c in range(3):
        out[c] = color[c]
    out[3] = one_minus_exp(s * -LN2)

    def left(k, c):
        for j in range(group):
            to, send = copy(k, j)
            pl.when(to != me)(send.wait_send)
        return c

    lax.fori_loop(0, units, left, 0)


def on_device(volume, tf_index, tf_table):
    depth, rows, cols = volume.shape
    n = lax.axis_size("depth")
    m = lax.axis_size("col")
    vm = pl.BlockSpec(memory_space=pltpu.VMEM)
    rb = rows // n
    units, group = rows // UNIT, UNIT // rb
    return pl.pallas_call(
        functools.partial(kernel, n, m),
        out_shape=jax.ShapeDtypeStruct((4, rb, cols), jnp.float32),
        in_specs=[pl.BlockSpec(memory_space=pltpu.HBM)] * 3,
        out_specs=vm,
        scratch_shapes=[
            pltpu.VMEM(volume.shape, volume.dtype),
            pltpu.VMEM(tf_index.shape, tf_index.dtype),
            pltpu.VMEM(tf_table.shape, tf_table.dtype),
            pltpu.SemaphoreType.DMA((2 + units,)),
            pltpu.VMEM((depth + 2, rows + 2 * PAD, cols), jnp.float32),
            pltpu.VMEM((units, 3, depth, UNIT, cols), jnp.float32),
            *[pltpu.VMEM((units, depth, UNIT, cols), jnp.float32)] * 3,
            pltpu.VMEM((units, 3, UNIT, cols), jnp.float32),
            pltpu.VMEM((units, UNIT, cols), jnp.float32),
            pltpu.VMEM((units, group, 4 * rb, cols), jnp.bfloat16),
            pltpu.VMEM((n, 4 * rb, cols), jnp.bfloat16),
            *[pltpu.VMEM((rows, cols), jnp.bfloat16)] * 5,
            pltpu.VMEM((rows, cols), jnp.float32),
            pltpu.SemaphoreType.DMA((units, group)),
            pltpu.SemaphoreType.DMA((n,)),
            pltpu.SemaphoreType.DMA((4,)),
            pltpu.SemaphoreType.DMA((4,)),
        ],
        compiler_params=pltpu.CompilerParams(
            collective_id=0, has_side_effects=True, vmem_limit_bytes=53 * 1024 * 1024),
    )(volume, tf_index, tf_table)


def solution(mesh):
    in_specs = (P("depth", None, "col"), P("depth", None, "col"), P())
    out_specs = P(None, "depth", "col")
    return jax.shard_map(
        on_device, mesh=mesh, in_specs=in_specs, out_specs=out_specs, check_vma=False
    )
```

time: 15.5 us -> 15.5 us (level)
  no operation moved by 1% of the time
where the time goes in v2:
time: 15.5 us; the launch traced here: 15.3 us
  Pallas kernels  14 us (90%)
  local copies, waits for them, and re-layouts  1.31 us (8%)
    pallas_call x1, Pallas kernels, on_device(): pl.pallas_call(functools.partial(kernel, n, m), out_shape=jax.ShapeDtypeS...  14 us
    unnamed x3, local copies, waits for them, and re-layouts  1.31 us

profile of v2, /device:TPU:0, one launch (start us, length us, event | category | flops | bytes accessed | tf_op | source)
XLA Modules:
  0.0 15.3 jit_solution(8775079451104777047)
XLA Ops:
  0.0 0.0 copy-start
  0.0 0.7 %copy-done = bf16[4,256]{1,0:T(4,128)(2,1)S(1)} copy-done((bf16[4,256]{1,0:T(4,128)(2,1)S(1)}, bf16[4,256]{1,0:T(4,128)(2,1)}, u32[]{:S(2)}) %copy-start) | copy-done | bytes 2072
  0.7 14.0 %shard_map.37 = f32[4,32,128]{2,1,0:T(8,128)S(1)} custom-call(bf16[16,256,128]{2,1,0:T(8,128)(2,1)} %vol_hbm.1, s32[16,256,128]{2,1,0:T(8,128)} %idx_hbm.1, bf16[4,256]{1,0:T(4,128)(2,1)S(1)} %copy-done), custom_call_target="tpu_custom_call" | custom-call | tf_op jit(solution)/shard_map/pallas_call | solution.py:285
  14.7 0.6 %copy.5 = f32[4,32,128]{2,1,0:T(8,128)} copy(f32[4,32,128]{2,1,0:T(8,128)S(1)} %shard_map.37) | data formatting | bytes 131072
Async XLA Ops:
  0.0 0.7 %copy-start = (bf16[4,256]{1,0:T(4,128)(2,1)S(1)}, bf16[4,256]{1,0:T(4,128)(2,1)}, u32[]{:S(2)}) copy-start(bf16[4,256]{1,0:T(4,128)(2,1)} %table_hbm.1) | copy-start | bytes 6148

commit v3 on v2

--- a/solution.py
+++ b/solution.py
@@ -13,6 +13,7 @@
 PAD = 8
 SUB = 8
 UNIT = 32
+CHUNKS = 4
 MESH = pl.DeviceIdType.MESH
 
 
@@ -24,7 +25,8 @@
 def place_of(k, mine, count):
     if count & (count - 1):
         return lax.rem(mine + 1 + k, count)
-    mask, out = count - 1 - k, 0
+    half = count // 2
+    mask, out = jnp.where(k < half, count - 1 - 2 * k, 2 * (count - 1 - k)), 0
     for i in range(count.bit_length() - 1):
         out = out + lax.rem(lax.div(mine, 1 << i) + lax.div(mask, 1 << i), 2) * (1 << i)
     return out
@@ -35,7 +37,7 @@
 
 
 def kernel(n, m, vol_hbm, idx_hbm, table_hbm, out, vol, idx, table, load_sem, fvol, weight, across, slope, square, base, depths,
-           part, recv, edge, zlo, zhi, from_left, from_right, halo, send_sem, recv_sem, halo_send, halo_recv):
+           part, other, mix, recv, edge, from_left, from_right, zlo, zhi, halo, pair_send, pair_recv, send_sem, recv_sem, halo_send, halo_recv):
     depth, rows, cols = vol.shape
     rb = rows // n
     group = UNIT // rb
@@ -47,10 +49,13 @@
 
     def load_labels(k):
         at = pl.ds(pl.multiple_of(place_of(k, my_unit, units) * UNIT, UNIT), UNIT)
-        return pltpu.make_async_copy(idx_hbm.at[:, at], idx.at[:, at], load_sem.at[2 + k])
-
-    loads = [pltpu.make_async_copy(src, dst, load_sem.at[i]) for i, (src, dst) in
-             enumerate(((table_hbm, table), (vol_hbm, vol)))]
+        return pltpu.make_async_copy(idx_hbm.at[:, at], idx.at[:, at], load_sem.at[k])
+
+    step = depth // CHUNKS
+    loads = [pltpu.make_async_copy(table_hbm, table, load_sem.at[units])]
+    for i in range(CHUNKS):
+        at = pl.ds(i * step, step)
+        loads.append(pltpu.make_async_copy(vol_hbm.at[at], vol.at[at], load_sem.at[units + 1 + i]))
     for load in loads:
         load.start()
     lax.fori_loop(0, units, lambda k, c: (load_labels(k).start(), c)[1], 0)
@@ -107,7 +112,15 @@
     sigma_middle = jnp.broadcast_to(middle[3], (SUB, cols))
     scale = [jnp.broadcast_to(jnp.exp2(o), (SUB, cols)) for o in middle[:3]]
 
-    loads[1].wait()
+    def widen(z, c):
+        fvol[z + 1, :PAD] = zero
+        fvol[z + 1, PAD + rows:] = zero
+        fvol[z + 1, PAD:PAD + rows] = vol[z].astype(jnp.float32)
+        return c
+
+    for i in range(CHUNKS):
+        loads[1 + i].wait()
+        lax.fori_loop(i * step, (i + 1) * step, widen, 0)
 
     def pick(z, total):
         at = jnp.where((r_i == cols - 1) & (c_i == z), 1.0, 0.0)
@@ -115,15 +128,12 @@
         return total + jnp.dot(vol[z], at.astype(jnp.bfloat16), preferred_element_type=jnp.float32)
 
     edges = lax.fori_loop(0, depth, pick, jnp.zeros((rows, cols), jnp.float32), unroll=True)
-    edge[...] = edges.astype(jnp.bfloat16)
-
-    def widen(z, c):
-        fvol[z + 1, :PAD] = zero
-        fvol[z + 1, PAD + rows:] = zero
-        fvol[z + 1, PAD:PAD + rows] = vol[z].astype(jnp.float32)
-        return c
-
-    lax.fori_loop(0, depth, widen, 0)
+    fold = cols // (2 * depth)
+    short = rows // fold
+    packed = edges[:short]
+    for i in range(1, fold):
+        packed = packed + pltpu.roll(edges[i * short:(i + 1) * short], 2 * depth * i, 1)
+    edge[...] = packed.astype(jnp.bfloat16)
 
     def look(k, c):
         @pl.when(k == 1)
@@ -203,18 +213,56 @@
 
     fvol[0, PAD:PAD + rows] = zlo[...].astype(jnp.float32)
     fvol[depth + 1, PAD:PAD + rows] = zhi[...].astype(jnp.float32)
-    lane = lax.broadcasted_iota(jnp.int32, (rows, cols), 1)
-    halo[...] = jnp.where(lane < depth, -from_left[...].astype(jnp.float32),
-                          jnp.where(lane < 2 * depth, from_right[...].astype(jnp.float32), 0.0))
+    lane = lax.broadcasted_iota(jnp.int32, (short, cols), 1)
+    packed = jnp.where(lax.rem(lane, 2 * depth) < depth, -from_left[...].astype(jnp.float32),
+                       from_right[...].astype(jnp.float32))
+    for i in range(fold):
+        mine_here = pltpu.roll(packed, cols - 2 * depth * i, 1) if i else packed
+        halo[i * short:(i + 1) * short] = jnp.where(lane < 2 * depth, mine_here, 0.0)
     lane = lax.broadcasted_iota(jnp.int32, (SUB, cols), 1)
 
-    def copy(k, j):
-        to = place_of(k, my_unit, units) * group + j
-        return to, pltpu.make_async_remote_copy(
-            src_ref=part.at[k, j], dst_ref=recv.at[me], send_sem=send_sem.at[k, j], recv_sem=recv_sem.at[me],
+    odd = lax.rem(me, 2)
+    partner = me + 1 - 2 * odd
+    behind = odd.astype(jnp.float32)
+    pairs = n // 2
+    my_pair = lax.div(me, 2)
+
+    def block_of(k, j):
+        return place_of(k, my_unit, units) * group + j
+
+    def hand_over(k, j):
+        slot = lax.div(block_of(k, j), 2)
+        return pltpu.make_async_remote_copy(
+            src_ref=part.at[k, j], dst_ref=other.at[slot], send_sem=pair_send.at[slot], recv_sem=pair_recv.at[slot],
+            device_id={"depth": partner}, device_id_type=MESH)
+
+    def deliver(to):
+        slot = lax.div(to, 2)
+        return pltpu.make_async_remote_copy(
+            src_ref=mix.at[slot], dst_ref=recv.at[my_pair], send_sem=send_sem.at[slot], recv_sem=recv_sem.at[my_pair],
             device_id={"depth": to}, device_id_type=MESH)
 
-    def shade(k, c):
+    def merge(k, j, own):
+        to = block_of(k, j)
+        slot = lax.div(to, 2)
+        hand_over(k, j).wait_recv()
+        theirs = other[slot].astype(jnp.float32)
+        theirs = [theirs[c * rb:(c + 1) * rb] for c in range(4)]
+        front = jnp.exp2(theirs[3] * behind)
+        back = jnp.exp2(own[3] * (1.0 - behind))
+        both = [own[c] * front + theirs[c] * back for c in range(3)] + [own[3] + theirs[3]]
+        both = jnp.concatenate(both, 0).astype(jnp.bfloat16)
+
+        @pl.when(to != me)
+        def _():
+            mix[slot] = both
+            deliver(to).start()
+
+        @pl.when(to == me)
+        def _():
+            recv[my_pair] = both
+
+    def shade(k):
         u0 = pl.multiple_of(place_of(k, my_unit, units) * UNIT, UNIT)
         sums = [[base[k, c3, i * SUB:(i + 1) * SUB] for c3 in range(3)] for i in range(tiles)]
         ends = [halo[pl.ds(u0 + i * SUB, SUB)] for i in range(tiles)]
@@ -233,25 +281,47 @@
                 lit = jnp.abs(facing) * lax.rsqrt(norm)
                 sums[i] = [a + weight[k, c3, z, r] * lit for c3, a in enumerate(sums[i])]
         color = [jnp.concatenate([sums[i][c3] * scale[c3] for i in range(tiles)], 0) for c3 in range(3)]
-        color.append(depths[k])
+        return color + [depths[k]]
+
+    def give(k, c):
+        color = shade(k)
         for j in range(group):
             part[k, j] = jnp.concatenate([v[j * rb:(j + 1) * rb] for v in color], 0).astype(jnp.bfloat16)
-            to, send = copy(k, j)
-            pl.when(to != me)(send.start)
-        return c
-
-    lax.fori_loop(0, units, shade, 0)
-    recv[me] = part[units - 1, lax.rem(me, group)]
+            if paired:
+                hand_over(k, j).start()
+            else:
+                pl.when(lax.rem(block_of(k, j) + me, 2) == 1)(hand_over(k, j).start)
+        return c
+
+    def keep(k, c):
+        merge(k, 0, shade(k))
+        return c
+
+    def gather_pair(k, c):
+        for j in range(group):
+            @pl.when(lax.rem(block_of(k, j) + me, 2) == 0)
+            def _():
+                own = part[k, j].astype(jnp.float32)
+                merge(k, j, [own[c3 * rb:(c3 + 1) * rb] for c3 in range(4)])
+        return c
+
+    paired = group == 1 and units & (units - 1) == 0
+    if paired:
+        lax.fori_loop(0, units // 2, give, 0)
+        lax.fori_loop(units // 2, units, keep, 0)
+    else:
+        lax.fori_loop(0, units, give, 0)
+        lax.fori_loop(0, units, gather_pair, 0)
 
     def arrive(k, c):
-        @pl.when(k != me)
+        @pl.when(k != my_pair)
         def _():
             pltpu.make_async_remote_copy(
-                src_ref=part.at[0, 0], dst_ref=recv.at[k], send_sem=send_sem.at[0, 0], recv_sem=recv_sem.at[k],
-                device_id={"depth": k}, device_id_type=MESH).wait_recv()
-        return c
-
-    lax.fori_loop(0, n, arrive, 0)
+                src_ref=mix.at[0], dst_ref=recv.at[k], send_sem=send_sem.at[0], recv_sem=recv_sem.at[k],
+                device_id={"depth": 2 * k + odd}, device_id_type=MESH).wait_recv()
+        return c
+
+    lax.fori_loop(0, pairs, arrive, 0)
 
     def over(j, carry):
         color, s = carry
@@ -261,18 +331,22 @@
         return color, s + piece[3 * rb:]
 
     init = jnp.zeros((rb, cols), jnp.float32)
-    color, s = lax.fori_loop(0, n, over, ((init,) * 3, init), unroll=8)
+    color, s = lax.fori_loop(0, pairs, over, ((init,) * 3, init), unroll=4)
     for c in range(3):
         out[c] = color[c]
     out[3] = one_minus_exp(s * -LN2)
 
-    def left(k, c):
-        for j in range(group):
-            to, send = copy(k, j)
-            pl.when(to != me)(send.wait_send)
-        return c
-
-    lax.fori_loop(0, units, left, 0)
+    def left(slot, c):
+        pltpu.make_async_remote_copy(
+            src_ref=part.at[0, 0], dst_ref=other.at[slot], send_sem=pair_send.at[slot], recv_sem=pair_recv.at[slot],
+            device_id={"depth": partner}, device_id_type=MESH).wait_send()
+
+        @pl.when(slot != my_pair)
+        def _():
+            deliver(2 * slot + odd).wait_send()
+        return c
+
+    lax.fori_loop(0, pairs, left, 0)
 
 
 def on_device(volume, tf_index, tf_table):
@@ -291,18 +365,18 @@
             pltpu.VMEM(volume.shape, volume.dtype),
             pltpu.VMEM(tf_index.shape, tf_index.dtype),
             pltpu.VMEM(tf_table.shape, tf_table.dtype),
-            pltpu.SemaphoreType.DMA((2 + units,)),
+            pltpu.SemaphoreType.DMA((units + 1 + CHUNKS,)),
             pltpu.VMEM((depth + 2, rows + 2 * PAD, cols), jnp.float32),
             pltpu.VMEM((units, 3, depth, UNIT, cols), jnp.float32),
             *[pltpu.VMEM((units, depth, UNIT, cols), jnp.float32)] * 3,
             pltpu.VMEM((units, 3, UNIT, cols), jnp.float32),
             pltpu.VMEM((units, UNIT, cols), jnp.float32),
             pltpu.VMEM((units, group, 4 * rb, cols), jnp.bfloat16),
-            pltpu.VMEM((n, 4 * rb, cols), jnp.bfloat16),
-            *[pltpu.VMEM((rows, cols), jnp.bfloat16)] * 5,
+            *[pltpu.VMEM((n // 2, 4 * rb, cols), jnp.bfloat16)] * 3,
+            *[pltpu.VMEM((2 * rows * depth // cols, cols), jnp.bfloat16)] * 3,
+            *[pltpu.VMEM((rows, cols), jnp.bfloat16)] * 2,
             pltpu.VMEM((rows, cols), jnp.float32),
-            pltpu.SemaphoreType.DMA((units, group)),
-            pltpu.SemaphoreType.DMA((n,)),
+            *[pltpu.SemaphoreType.DMA((n // 2,))] * 4,
             pltpu.SemaphoreType.DMA((4,)),
             pltpu.SemaphoreType.DMA((4,)),
         ],

time: 15.5 us -> 14.9 us (0.961)
  Pallas kernels: 14 us -> 13.4 us
    pallas_call x1, Pallas kernels: 14 us -> 13.4 us  [on_device(): pl.pallas_call(functools.partial(kernel, n, m), out_shape=jax.ShapeDtypeS...]
where the time goes in v3:
time: 14.9 us; the launch traced here: 14.7 us
  Pallas kernels  13.4 us (90%)
  local copies, waits for them, and re-layouts  1.31 us (9%)
    pallas_call x1, Pallas kernels, on_device(): pl.pallas_call(functools.partial(kernel, n, m), out_shape=jax.ShapeDtypeS...  13.4 us
    unnamed x3, local copies, waits for them, and re-layouts  1.31 us

profile of v3, /device:TPU:0, one launch (start us, length us, event | category | flops | bytes accessed | tf_op | source)
XLA Modules:
  0.0 14.7 jit_solution(10224313245042073984)
XLA Ops:
  0.0 0.0 copy-start
  0.0 0.7 %copy-done = bf16[4,256]{1,0:T(4,128)(2,1)S(1)} copy-done((bf16[4,256]{1,0:T(4,128)(2,1)S(1)}, bf16[4,256]{1,0:T(4,128)(2,1)}, u32[]{:S(2)}) %copy-start) | copy-done | bytes 2072
  0.7 13.4 %shard_map.37 = f32[4,32,128]{2,1,0:T(8,128)S(1)} custom-call(bf16[16,256,128]{2,1,0:T(8,128)(2,1)} %vol_hbm.1, s32[16,256,128]{2,1,0:T(8,128)} %idx_hbm.1, bf16[4,256]{1,0:T(4,128)(2,1)S(1)} %copy-done), custom_call_target="tpu_custom_call" | custom-call | tf_op jit(solution)/shard_map/pallas_call | solution.py:359
  14.1 0.6 %copy.5 = f32[4,32,128]{2,1,0:T(8,128)} copy(f32[4,32,128]{2,1,0:T(8,128)S(1)} %shard_map.37) | data formatting | bytes 131072
Async XLA Ops:
  0.0 0.7 %copy-start = (bf16[4,256]{1,0:T(4,128)(2,1)S(1)}, bf16[4,256]{1,0:T(4,128)(2,1)}, u32[]{:S(2)}) copy-start(bf16[4,256]{1,0:T(4,128)(2,1)} %table_hbm.1) | copy-start | bytes 6148

commit v4 on v3

--- a/solution.py
+++ b/solution.py
@@ -58,7 +58,6 @@
         loads.append(pltpu.make_async_copy(vol_hbm.at[at], vol.at[at], load_sem.at[units + 1 + i]))
     for load in loads:
         load.start()
-    lax.fori_loop(0, units, lambda k, c: (load_labels(k).start(), c)[1], 0)
 
     barrier = pltpu.get_barrier_semaphore()
 
@@ -66,21 +65,23 @@
         pl.semaphore_signal(barrier, inc=1, device_id={"depth": lax.rem(me + 1 + k, n)}, device_id_type=MESH)
         return c
 
-    lax.fori_loop(0, n - 1, greet, 0)
+    lax.fori_loop(0, n - 1, greet, 0, unroll=True)
     for there, side in ((mine > 0, -1), (mine < m - 1, 1)):
         @pl.when(there)
         def _():
             pl.semaphore_signal(barrier, inc=1, device_id={"col": mine + side}, device_id_type=MESH)
+
+    lax.fori_loop(0, units, lambda k, c: (load_labels(k).start(), c)[1], 0, unroll=True)
 
     def halo_copy(k, src, dst, axis, to):
         return pltpu.make_async_remote_copy(
             src_ref=src, dst_ref=dst, send_sem=halo_send.at[k], recv_sem=halo_recv.at[k],
             device_id={axis: to}, device_id_type=MESH)
 
-    halos = ((mine > 0, mine < m - 1, halo_copy(2, edge, from_right, "col", mine - 1), from_right),
-             (mine < m - 1, mine > 0, halo_copy(3, edge, from_left, "col", mine + 1), from_left),
-             (me > 0, me < n - 1, halo_copy(0, vol.at[0], zhi, "depth", me - 1), zhi),
-             (me < n - 1, me > 0, halo_copy(1, vol.at[depth - 1], zlo, "depth", me + 1), zlo))
+    halos = ((me > 0, me < n - 1, halo_copy(0, vol.at[0], zhi, "depth", me - 1), zhi),
+             (me < n - 1, me > 0, halo_copy(1, vol.at[depth - 1], zlo, "depth", me + 1), zlo),
+             (mine > 0, mine < m - 1, halo_copy(2, edge, from_right, "col", mine - 1), from_right),
+             (mine < m - 1, mine > 0, halo_copy(3, edge, from_left, "col", mine + 1), from_left))
 
     r_i = lax.broadcasted_iota(jnp.int32, (cols, cols), 0)
     c_i = lax.broadcasted_iota(jnp.int32, (cols, cols), 1)
@@ -127,17 +128,20 @@
         at = at + jnp.where((r_i == 0) & (c_i == depth + z), 1.0, 0.0)
         return total + jnp.dot(vol[z], at.astype(jnp.bfloat16), preferred_element_type=jnp.float32)
 
-    edges = lax.fori_loop(0, depth, pick, jnp.zeros((rows, cols), jnp.float32), unroll=True)
     fold = cols // (2 * depth)
     short = rows // fold
-    packed = edges[:short]
-    for i in range(1, fold):
-        packed = packed + pltpu.roll(edges[i * short:(i + 1) * short], 2 * depth * i, 1)
-    edge[...] = packed.astype(jnp.bfloat16)
+
+    def pack_edges():
+        edges = lax.fori_loop(0, depth, pick, jnp.zeros((rows, cols), jnp.float32), unroll=True)
+        packed = edges[:short]
+        for i in range(1, fold):
+            packed = packed + pltpu.roll(edges[i * short:(i + 1) * short], 2 * depth * i, 1)
+        edge[...] = packed.astype(jnp.bfloat16)
 
     def look(k, c):
         @pl.when(k == 1)
         def _():
+            pack_edges()
             neighbours = (mine > 0).astype(jnp.int32) + (mine < m - 1).astype(jnp.int32)
             pl.semaphore_wait(barrier, n - 1 + neighbours)
             for sends, _, copy, _ in halos:
@@ -246,8 +250,7 @@
         to = block_of(k, j)
         slot = lax.div(to, 2)
         hand_over(k, j).wait_recv()
-        theirs = other[slot].astype(jnp.float32)
-        theirs = [theirs[c * rb:(c + 1) * rb] for c in range(4)]
+        theirs = [other[slot, c * rb:(c + 1) * rb] for c in range(4)]
         front = jnp.exp2(theirs[3] * behind)
         back = jnp.exp2(own[3] * (1.0 - behind))
         both = [own[c] * front + theirs[c] * back for c in range(3)] + [own[3] + theirs[3]]
@@ -286,7 +289,7 @@
     def give(k, c):
         color = shade(k)
         for j in range(group):
-            part[k, j] = jnp.concatenate([v[j * rb:(j + 1) * rb] for v in color], 0).astype(jnp.bfloat16)
+            part[k, j] = jnp.concatenate([v[j * rb:(j + 1) * rb] for v in color], 0)
             if paired:
                 hand_over(k, j).start()
             else:
@@ -301,8 +304,7 @@
         for j in range(group):
             @pl.when(lax.rem(block_of(k, j) + me, 2) == 0)
             def _():
-                own = part[k, j].astype(jnp.float32)
-                merge(k, j, [own[c3 * rb:(c3 + 1) * rb] for c3 in range(4)])
+                merge(k, j, [part[k, j, c3 * rb:(c3 + 1) * rb] for c3 in range(4)])
         return c
 
     paired = group == 1 and units & (units - 1) == 0
@@ -371,8 +373,9 @@
             *[pltpu.VMEM((units, depth, UNIT, cols), jnp.float32)] * 3,
             pltpu.VMEM((units, 3, UNIT, cols), jnp.float32),
             pltpu.VMEM((units, UNIT, cols), jnp.float32),
-            pltpu.VMEM((units, group, 4 * rb, cols), jnp.bfloat16),
-            *[pltpu.VMEM((n // 2, 4 * rb, cols), jnp.bfloat16)] * 3,
+            pltpu.VMEM((units, group, 4 * rb, cols), jnp.float32),
+            pltpu.VMEM((n // 2, 4 * rb, cols), jnp.float32),
+            *[pltpu.VMEM((n // 2, 4 * rb, cols), jnp.bfloat16)] * 2,
             *[pltpu.VMEM((2 * rows * depth // cols, cols), jnp.bfloat16)] * 3,
             *[pltpu.VMEM((rows, cols), jnp.bfloat16)] * 2,
             pltpu.VMEM((rows, cols), jnp.float32),

time: 14.9 us -> 14.9 us (level)
  no operation moved by 1% of the time
where the time goes in v4:
time: 14.9 us; the launch traced here: 14.8 us
  Pallas kernels  13.4 us (90%)
  local copies, waits for them, and re-layouts  1.31 us (9%)
    pallas_call x1, Pallas kernels, on_device(): pl.pallas_call(functools.partial(kernel, n, m), out_shape=jax.ShapeDtypeS...  13.4 us
    unnamed x3, local copies, waits for them, and re-layouts  1.31 us

profile of v4, /device:TPU:0, one launch (start us, length us, event | category | flops | bytes accessed | tf_op | source)
XLA Modules:
  0.0 14.8 jit_solution(6900939350918463281)
XLA Ops:
  0.0 0.0 copy-start
  0.0 0.7 %copy-done = bf16[4,256]{1,0:T(4,128)(2,1)S(1)} copy-done((bf16[4,256]{1,0:T(4,128)(2,1)S(1)}, bf16[4,256]{1,0:T(4,128)(2,1)}, u32[]{:S(2)}) %copy-start) | copy-done | bytes 2072
  0.7 13.4 %shard_map.37 = f32[4,32,128]{2,1,0:T(8,128)S(1)} custom-call(bf16[16,256,128]{2,1,0:T(8,128)(2,1)} %vol_hbm.1, s32[16,256,128]{2,1,0:T(8,128)} %idx_hbm.1, bf16[4,256]{1,0:T(4,128)(2,1)S(1)} %copy-done), custom_call_target="tpu_custom_call" | custom-call | tf_op jit(solution)/shard_map/pallas_call | solution.py:361
  14.1 0.6 %copy.5 = f32[4,32,128]{2,1,0:T(8,128)} copy(f32[4,32,128]{2,1,0:T(8,128)S(1)} %shard_map.37) | data formatting | bytes 131072
Async XLA Ops:
  0.0 0.7 %copy-start = (bf16[4,256]{1,0:T(4,128)(2,1)S(1)}, bf16[4,256]{1,0:T(4,128)(2,1)}, u32[]{:S(2)}) copy-start(bf16[4,256]{1,0:T(4,128)(2,1)} %table_hbm.1) | copy-start | bytes 6148

commit v5 on v4

--- a/solution.py
+++ b/solution.py
@@ -47,8 +47,11 @@
     mine = lax.axis_index("col")
     my_unit = lax.div(me, group)
 
-    def load_labels(k):
-        at = pl.ds(pl.multiple_of(place_of(k, my_unit, units) * UNIT, UNIT), UNIT)
+    def start_of(k):
+        return place_of(jnp.minimum(k, units - 1), my_unit, units) * UNIT
+
+    def load_labels(k, start):
+        at = pl.ds(pl.multiple_of(start, UNIT), UNIT)
         return pltpu.make_async_copy(idx_hbm.at[:, at], idx.at[:, at], load_sem.at[k])
 
     step = depth // CHUNKS
@@ -71,7 +74,7 @@
         def _():
             pl.semaphore_signal(barrier, inc=1, device_id={"col": mine + side}, device_id_type=MESH)
 
-    lax.fori_loop(0, units, lambda k, c: (load_labels(k).start(), c)[1], 0, unroll=True)
+    lax.fori_loop(0, units, lambda k, c: (load_labels(k, start_of(k)).start(), c)[1], 0, unroll=True)
 
     def halo_copy(k, src, dst, axis, to):
         return pltpu.make_async_remote_copy(
@@ -138,7 +141,7 @@
             packed = packed + pltpu.roll(edges[i * short:(i + 1) * short], 2 * depth * i, 1)
         edge[...] = packed.astype(jnp.bfloat16)
 
-    def look(k, c):
+    def look(k, start):
         @pl.when(k == 1)
         def _():
             pack_edges()
@@ -147,8 +150,8 @@
             for sends, _, copy, _ in halos:
                 pl.when(sends)(copy.start)
 
-        load_labels(k).wait()
-        u0 = pl.multiple_of(place_of(k, my_unit, units) * UNIT, UNIT)
+        load_labels(k, start).wait()
+        u0 = pl.multiple_of(start, UNIT)
         sums = [[jnp.zeros((SUB, cols), jnp.float32) for _ in range(4)] for _ in range(tiles)]
         def decode(z, i, first, second, gxs):
             r = slice(i * SUB, (i + 1) * SUB)
@@ -203,9 +206,9 @@
             for c3 in range(3):
                 base[k, c3, r] = sums[i][c3] * 0.25
             depths[k, r] = sums[i][3]
-        return c
-
-    lax.fori_loop(0, units, look, 0)
+        return start_of(k + 1)
+
+    lax.fori_loop(0, units, look, start_of(0))
 
     for sends, receives, copy, landed in halos:
         pl.when(sends)(copy.wait_send)
@@ -265,8 +268,8 @@
         def _():
             recv[my_pair] = both
 
-    def shade(k):
-        u0 = pl.multiple_of(place_of(k, my_unit, units) * UNIT, UNIT)
+    def shade(k, start):
+        u0 = pl.multiple_of(start, UNIT)
         sums = [[base[k, c3, i * SUB:(i + 1) * SUB] for c3 in range(3)] for i in range(tiles)]
         ends = [halo[pl.ds(u0 + i * SUB, SUB)] for i in range(tiles)]
         for z in range(depth):
@@ -286,19 +289,19 @@
         color = [jnp.concatenate([sums[i][c3] * scale[c3] for i in range(tiles)], 0) for c3 in range(3)]
         return color + [depths[k]]
 
-    def give(k, c):
-        color = shade(k)
+    def give(k, start):
+        color = shade(k, start)
         for j in range(group):
             part[k, j] = jnp.concatenate([v[j * rb:(j + 1) * rb] for v in color], 0)
             if paired:
                 hand_over(k, j).start()
             else:
                 pl.when(lax.rem(block_of(k, j) + me, 2) == 1)(hand_over(k, j).start)
-        return c
-
-    def keep(k, c):
-        merge(k, 0, shade(k))
-        return c
+        return start_of(k + 1)
+
+    def keep(k, start):
+        merge(k, 0, shade(k, start))
+        return start_of(k + 1)
 
     def gather_pair(k, c):
         for j in range(group):
@@ -309,10 +312,10 @@
 
     paired = group == 1 and units & (units - 1) == 0
     if paired:
-        lax.fori_loop(0, units // 2, give, 0)
-        lax.fori_loop(units // 2, units, keep, 0)
+        start = lax.fori_loop(0, units // 2, give, start_of(0))
+        lax.fori_loop(units // 2, units, keep, start)
     else:
-        lax.fori_loop(0, units, give, 0)
+        lax.fori_loop(0, units, give, start_of(0))
         lax.fori_loop(0, units, gather_pair, 0)
 
     def arrive(k, c):

time: 14.9 us -> 14.9 us (level)
  no operation moved by 1% of the time
where the time goes in v5:
time: 14.9 us; the launch traced here: 14.7 us
  Pallas kernels  13.4 us (90%)
  local copies, waits for them, and re-layouts  1.31 us (9%)
    pallas_call x1, Pallas kernels, on_device(): pl.pallas_call(functools.partial(kernel, n, m), out_shape=jax.ShapeDtypeS...  13.4 us
    unnamed x3, local copies, waits for them, and re-layouts  1.31 us

profile of v5, /device:TPU:0, one launch (start us, length us, event | category | flops | bytes accessed | tf_op | source)
XLA Modules:
  0.0 14.7 jit_solution(3505376326904634086)
XLA Ops:
  0.0 0.0 copy-start
  0.0 0.7 %copy-done = bf16[4,256]{1,0:T(4,128)(2,1)S(1)} copy-done((bf16[4,256]{1,0:T(4,128)(2,1)S(1)}, bf16[4,256]{1,0:T(4,128)(2,1)}, u32[]{:S(2)}) %copy-start) | copy-done | bytes 2072
  0.7 13.4 %shard_map.37 = f32[4,32,128]{2,1,0:T(8,128)S(1)} custom-call(bf16[16,256,128]{2,1,0:T(8,128)(2,1)} %vol_hbm.1, s32[16,256,128]{2,1,0:T(8,128)} %idx_hbm.1, bf16[4,256]{1,0:T(4,128)(2,1)S(1)} %copy-done), custom_call_target="tpu_custom_call" | custom-call | tf_op jit(solution)/shard_map/pallas_call | solution.py:364
  14.1 0.6 %copy.5 = f32[4,32,128]{2,1,0:T(8,128)} copy(f32[4,32,128]{2,1,0:T(8,128)S(1)} %shard_map.37) | data formatting | bytes 131072
Async XLA Ops:
  0.0 0.7 %copy-start = (bf16[4,256]{1,0:T(4,128)(2,1)S(1)}, bf16[4,256]{1,0:T(4,128)(2,1)}, u32[]{:S(2)}) copy-start(bf16[4,256]{1,0:T(4,128)(2,1)} %table_hbm.1) | copy-start | bytes 6148

commit v6 on v5

--- a/solution.py
+++ b/solution.py
@@ -37,7 +37,7 @@
 
 
 def kernel(n, m, vol_hbm, idx_hbm, table_hbm, out, vol, idx, table, load_sem, fvol, weight, across, slope, square, base, depths,
-           part, other, mix, recv, edge, from_left, from_right, zlo, zhi, halo, pair_send, pair_recv, send_sem, recv_sem, halo_send, halo_recv):
+           part, other, mix, recv, edge, from_left, from_right, zlo, zhi, halo, pair_send, pair_recv, send_sem, recv_sem, halo_send, halo_recv, vouched):
     depth, rows, cols = vol.shape
     rb = rows // n
     group = UNIT // rb
@@ -64,11 +64,25 @@
 
     barrier = pltpu.get_barrier_semaphore()
 
-    def greet(k, c):
-        pl.semaphore_signal(barrier, inc=1, device_id={"depth": lax.rem(me + 1 + k, n)}, device_id_type=MESH)
-        return c
-
-    lax.fori_loop(0, n - 1, greet, 0, unroll=True)
+    odd = lax.rem(me, 2)
+    cube = n == 8
+
+    def across_bit(i):
+        return me + (1 - 2 * lax.rem(lax.div(me, 1 << i), 2)) * (1 << i)
+
+    def greet(to):
+        pl.semaphore_signal(barrier, inc=1, device_id={"depth": to}, device_id_type=MESH)
+
+    beside = me - 1 + 2 * odd
+    has_beside = jnp.where(odd == 1, me < n - 1, me > 0)
+    if cube:
+        for i in range(3):
+            greet(across_bit(i))
+        pl.when(has_beside)(lambda: greet(beside))
+        greeted = 3 + has_beside.astype(jnp.int32)
+    else:
+        lax.fori_loop(0, n - 1, lambda k, c: (greet(lax.rem(me + 1 + k, n)), c)[1], 0)
+        greeted = n - 1
     for there, side in ((mine > 0, -1), (mine < m - 1, 1)):
         @pl.when(there)
         def _():
@@ -146,7 +160,9 @@
         def _():
             pack_edges()
             neighbours = (mine > 0).astype(jnp.int32) + (mine < m - 1).astype(jnp.int32)
-            pl.semaphore_wait(barrier, n - 1 + neighbours)
+            pl.semaphore_wait(barrier, greeted + neighbours)
+            if cube:
+                pl.semaphore_signal(vouched, inc=1, device_id={"depth": across_bit(1)}, device_id_type=MESH)
             for sends, _, copy, _ in halos:
                 pl.when(sends)(copy.start)
 
@@ -228,7 +244,6 @@
         halo[i * short:(i + 1) * short] = jnp.where(lane < 2 * depth, mine_here, 0.0)
     lane = lax.broadcasted_iota(jnp.int32, (SUB, cols), 1)
 
-    odd = lax.rem(me, 2)
     partner = me + 1 - 2 * odd
     behind = odd.astype(jnp.float32)
     pairs = n // 2
@@ -313,9 +328,13 @@
     paired = group == 1 and units & (units - 1) == 0
     if paired:
         start = lax.fori_loop(0, units // 2, give, start_of(0))
+        if cube:
+            pl.semaphore_wait(vouched, 1)
         lax.fori_loop(units // 2, units, keep, start)
     else:
         lax.fori_loop(0, units, give, start_of(0))
+        if cube:
+            pl.semaphore_wait(vouched, 1)
         lax.fori_loop(0, units, gather_pair, 0)
 
     def arrive(k, c):
@@ -385,6 +404,7 @@
             *[pltpu.SemaphoreType.DMA((n // 2,))] * 4,
             pltpu.SemaphoreType.DMA((4,)),
             pltpu.SemaphoreType.DMA((4,)),
+            pltpu.SemaphoreType.REGULAR,
         ],
         compiler_params=pltpu.CompilerParams(
             collective_id=0, has_side_effects=True, vmem_limit_bytes=53 * 1024 * 1024),

time: 14.9 us -> 14.9 us (level)
  no operation moved by 1% of the time
where the time goes in v6:
time: 14.9 us; the launch traced here: 14.7 us
  Pallas kernels  13.4 us (90%)
  local copies, waits for them, and re-layouts  1.31 us (9%)
    pallas_call x1, Pallas kernels, on_device(): pl.pallas_call(functools.partial(kernel, n, m), out_shape=jax.ShapeDtypeS...  13.4 us
    unnamed x3, local copies, waits for them, and re-layouts  1.31 us

profile of v6, /device:TPU:0, one launch (start us, length us, event | category | flops | bytes accessed | tf_op | source)
XLA Modules:
  0.0 14.7 jit_solution(7631701713924587591)
XLA Ops:
  0.0 0.0 copy-start
  0.0 0.7 %copy-done = bf16[4,256]{1,0:T(4,128)(2,1)S(1)} copy-done((bf16[4,256]{1,0:T(4,128)(2,1)S(1)}, bf16[4,256]{1,0:T(4,128)(2,1)}, u32[]{:S(2)}) %copy-start) | copy-done | bytes 2072
  0.7 13.4 %shard_map.37 = f32[4,32,128]{2,1,0:T(8,128)S(1)} custom-call(bf16[16,256,128]{2,1,0:T(8,128)(2,1)} %vol_hbm.1, s32[16,256,128]{2,1,0:T(8,128)} %idx_hbm.1, bf16[4,256]{1,0:T(4,128)(2,1)S(1)} %copy-done), custom_call_target="tpu_custom_call" | custom-call | tf_op jit(solution)/shard_map/pallas_call | solution.py:383
  14.1 0.6 %copy.5 = f32[4,32,128]{2,1,0:T(8,128)} copy(f32[4,32,128]{2,1,0:T(8,128)S(1)} %shard_map.37) | data formatting | bytes 131072
Async XLA Ops:
  0.0 0.7 %copy-start = (bf16[4,256]{1,0:T(4,128)(2,1)S(1)}, bf16[4,256]{1,0:T(4,128)(2,1)}, u32[]{:S(2)}) copy-start(bf16[4,256]{1,0:T(4,128)(2,1)} %table_hbm.1) | copy-start | bytes 6148

commit v7 on v5

--- a/solution.py
+++ b/solution.py
@@ -13,7 +13,7 @@
 PAD = 8
 SUB = 8
 UNIT = 32
-CHUNKS = 4
+CHUNKS = 2
 MESH = pl.DeviceIdType.MESH
 
 

time: 14.9 us -> 14.9 us (level)
  no operation moved by 1% of the time
where the time goes in v7:
time: 14.9 us; the launch traced here: 14.7 us
  Pallas kernels  13.4 us (90%)
  local copies, waits for them, and re-layouts  1.31 us (9%)
    pallas_call x1, Pallas kernels, on_device(): pl.pallas_call(functools.partial(kernel, n, m), out_shape=jax.ShapeDtypeS...  13.4 us
    unnamed x3, local copies, waits for them, and re-layouts  1.31 us

profile of v7, /device:TPU:0, one launch (start us, length us, event | category | flops | bytes accessed | tf_op | source)
XLA Modules:
  0.0 14.7 jit_solution(10090062368975787503)
XLA Ops:
  0.0 0.0 copy-start
  0.0 0.7 %copy-done = bf16[4,256]{1,0:T(4,128)(2,1)S(1)} copy-done((bf16[4,256]{1,0:T(4,128)(2,1)S(1)}, bf16[4,256]{1,0:T(4,128)(2,1)}, u32[]{:S(2)}) %copy-start) | copy-done | bytes 2072
  0.7 13.4 %shard_map.37 = f32[4,32,128]{2,1,0:T(8,128)S(1)} custom-call(bf16[16,256,128]{2,1,0:T(8,128)(2,1)} %vol_hbm.1, s32[16,256,128]{2,1,0:T(8,128)} %idx_hbm.1, bf16[4,256]{1,0:T(4,128)(2,1)S(1)} %copy-done), custom_call_target="tpu_custom_call" | custom-call | tf_op jit(solution)/shard_map/pallas_call | solution.py:364
  14.1 0.6 %copy.5 = f32[4,32,128]{2,1,0:T(8,128)} copy(f32[4,32,128]{2,1,0:T(8,128)S(1)} %shard_map.37) | data formatting | bytes 131072
Async XLA Ops:
  0.0 0.7 %copy-start = (bf16[4,256]{1,0:T(4,128)(2,1)S(1)}, bf16[4,256]{1,0:T(4,128)(2,1)}, u32[]{:S(2)}) copy-start(bf16[4,256]{1,0:T(4,128)(2,1)} %table_hbm.1) | copy-start | bytes 6148
